TPU v7x, 32 devices: a whole 2x2x4 slice. The times are simulated.
32 devices in a mesh: blk: 2 (over y), tiles: 16 (over z, x, core).
Axes of the slice: x: 2, y: 2, z: 4, core: 2. Of those that a mesh axis runs over, the one named last changes fastest.
Arguments:
- tensor_tiles: bfloat16 [2, 32, 64, 4096], P('blk', 'tiles'), may hold values from -6 to 6
- tile_iblock: int32 [2, 32], P('blk', 'tiles'), may hold values from 0 to 1
- tile_jslot: int32 [2, 32], P('blk', 'tiles'), may hold values from 0 to 1, as said below
- tile_kslot: int32 [2, 32], P('blk', 'tiles'), may hold values from 0 to 1, as said below
- block_jlist: int32 [2, 32], P('blk', 'tiles'), may hold values from 0 to 255, as said below
- block_klist: int32 [2, 32], P('blk', 'tiles'), may hold values from 0 to 63, as said below
- factor_b: bfloat16 [256, 64, 512], P(None, 'tiles'), may hold values from -0.5 to 0.5
- factor_c: bfloat16 [64, 64, 512], P(None, 'tiles'), may hold values from -0.75 to 0.75
Outputs:
- mttkrp: float32 [2048, 512], P(('blk', 'tiles'))
Inputs may be any that keep to these rules, and one draw needn't show every extreme that they name: `block_jlist`: the 2 entries of one device's list are distinct. `block_klist`: the 2 entries of one device's list are distinct. `tile_jslot`: one device's tiles use between 1 and 2 distinct positions, and all 2 on some device. `tile_kslot`: one device's tiles use between 1 and 2 distinct positions, and all 2 on some device.
All inputs are finite; a program needn't handle non-finite values.
Results may differ from a plain program's by a relative error of at most 0.011.
Values may be sent and summed in bfloat16 or wider, within the bound.
No kernel may reach another device: no remote copies, remote signals or barrier semaphores. Data moves between devices by JAX's collectives and lax.ppermute only.
A program may use at most 64 MiB of HBM per device.

v0:
```python
import jax
import jax.numpy as jnp
from jax import lax
from jax.experimental import pallas as pl
from jax.experimental.pallas import tpu as pltpu
from jax.sharding import PartitionSpec as P

MIB = 1024 * 1024
LANES = 128


def in_hbm(*arrays):
    return [pltpu.with_memory_space_constraint(array, pltpu.HBM) for array in arrays]


def make_requests(chips, owners, slots_two, slots_three, list_two, list_three, factor_b, factor_c):
    count = owners.shape[1]
    listed = list_two.shape[1]
    small = (owners, slots_two, slots_three, list_two, list_three)
    factors = (factor_b, factor_c)

    def kernel(*refs):
        sources, outs, held, sem = refs[:7], refs[7:10], refs[10:15], refs[15]
        copies = [
            pltpu.make_async_copy(source, target, sem.at[at])
            for at, (source, target) in enumerate(zip(sources, (*held, *outs[1:])))
        ]
        for copy in copies:
            copy.start()
        for copy in copies[:5]:
            copy.wait()
        own, slot_two, slot_three, two, three = held
        words = []
        for slot, table in ((slot_two, two), (slot_three, three)):
            for which in range(count):
                word = table[0, 0]
                for entry in range(1, listed):
                    word = jnp.where(slot[0, which] == entry, table[0, entry], word)
                words.append(word)
        words.extend(own[0, which] for which in range(count))
        lane = lax.broadcasted_iota(jnp.int32, (1, LANES), 1)
        row = jnp.zeros((1, LANES), jnp.int32)
        for at, word in enumerate(words):
            row = jnp.where(lane == at, word, row)
        for chip in range(chips):
            outs[0][chip] = row
        for copy in copies[5:]:
            copy.wait()

    return pl.pallas_call(
        kernel,
        out_shape=[jax.ShapeDtypeStruct((chips, 1, LANES), jnp.int32)]
        + [jax.ShapeDtypeStruct(factor.shape, factor.dtype) for factor in factors],
        in_specs=[pl.BlockSpec(memory_space=pltpu.HBM)] * 7,
        out_specs=[pl.BlockSpec(memory_space=pltpu.VMEM)] * 3,
        scratch_shapes=[pltpu.SMEM(array.shape, jnp.int32) for array in small] + [pltpu.SemaphoreType.DMA((7,))],
        compiler_params=pltpu.CompilerParams(vmem_limit_bytes=8 * MIB),
        name="make_requests",
    )(*in_hbm(*small, *factors))


def gather_rows(asked, count, mine, paired):
    chips = asked.shape[0]
    wants = 2 * count
    rows, rank = mine[0].shape[1:]

    def kernel(asked_ref, mine_b, mine_c, pair_b, pair_c, out_ref):
        side = lax.rem(lax.axis_index("tiles"), 2)
        for chip in range(chips):
            words = asked_ref[chip]
            for want in range(wants):
                own, other = (mine_b, pair_b) if want < count else (mine_c, pair_c)
                block = words[0, want]
                out_ref[chip, want, side] = own[block]
                out_ref[chip, want, 1 - side] = other[block]

    return pl.pallas_call(
        kernel,
        out_shape=jax.ShapeDtypeStruct((chips, wants, 2, rows, rank), mine[0].dtype),
        in_specs=[pl.BlockSpec(memory_space=pltpu.VMEM)] * 5,
        out_specs=pl.BlockSpec(memory_space=pltpu.VMEM),
        compiler_params=pltpu.CompilerParams(vmem_limit_bytes=8 * MIB),
        name="gather_rows",
    )(asked, *mine, *paired)


def contract(requests, fetched, order, tiles, groups):
    chips, wants, halves, rows, rank = fetched.shape
    count, inner, width = tiles.shape
    across = chips * halves * rows
    depth = width // across
    step = max(1, 1024 // depth)

    def kernel(requests_ref, fetched_ref, tiles_ref, own_ref, send_ref, factor_ref, index_ref, sem):
        copy = pltpu.make_async_copy(requests_ref.at[0], index_ref, sem)
        copy.start()
        me = lax.axis_index("blk")
        for want in range(wants):
            for came, chip in enumerate(order):
                for half in range(halves):
                    at = (chip * halves + half) * rows
                    factor_ref[want, at : at + rows, :] = fetched_ref[came, want, half].astype(jnp.float32)
        terms = []
        for which in range(count):
            mode_three = factor_ref[count + which].astype(jnp.bfloat16)
            term = jnp.zeros((inner, rank), jnp.float32)
            for start in range(0, across, step):
                product = jnp.concatenate(
                    [
                        jnp.broadcast_to(factor_ref[which, j : j + 1, :], (depth, rank)).astype(jnp.bfloat16)
                        * mode_three
                        for j in range(start, start + step)
                    ],
                    axis=0,
                )
                term = term + jnp.dot(
                    tiles_ref[which, :, start * depth : (start + step) * depth],
                    product,
                    preferred_element_type=jnp.float32,
                )
            terms.append(term)
        copy.wait()
        for shift in range(groups):
            group = lax.rem(me + shift, groups)
            total = jnp.zeros((inner, rank), jnp.float32)
            for which in range(count):
                total = total + jnp.where(index_ref[0, 2 * count + which] == group, terms[which], 0.0)
            rounded = total.astype(jnp.bfloat16)
            if shift == 0:
                own_ref[...] = rounded
            else:
                send_ref[shift - 1] = rounded

    return pl.pallas_call(
        kernel,
        out_shape=(
            jax.ShapeDtypeStruct((inner, rank), jnp.bfloat16),
            jax.ShapeDtypeStruct((groups - 1, inner, rank), jnp.bfloat16),
        ),
        in_specs=[
            pl.BlockSpec(memory_space=pl.ANY),
            pl.BlockSpec(memory_space=pltpu.VMEM),
            pl.BlockSpec(memory_space=pltpu.VMEM),
        ],
        out_specs=(pl.BlockSpec(memory_space=pltpu.VMEM), pl.BlockSpec(memory_space=pltpu.VMEM)),
        scratch_shapes=[
            pltpu.VMEM((wants, across, rank), jnp.float32),
            pltpu.SMEM((1, LANES), jnp.int32),
            pltpu.SemaphoreType.DMA,
        ],
        compiler_params=pltpu.CompilerParams(vmem_limit_bytes=16 * MIB),
        name="contract",
    )(requests, fetched, tiles)


def per_device(
    tensor_tiles, tile_iblock, tile_jslot, tile_kslot, block_jlist, block_klist, factor_b, factor_c
):
    groups = lax.axis_size("blk")
    size = lax.axis_size("tiles")
    chips = size // 2
    order = [(chip + chips // 2 + 1) % chips for chip in range(chips)]
    same_side = [[2 * chip + side for chip in order] for side in range(2)]
    count = tensor_tiles.shape[1]

    def exchange(array):
        return lax.all_to_all(
            array, "tiles", split_axis=0, concat_axis=0, tiled=True, axis_index_groups=same_side
        )

    requests, *mine = make_requests(
        chips, tile_iblock, tile_jslot, tile_kslot, block_jlist, block_klist, factor_b, factor_c
    )
    paired = [lax.ppermute(factor, "tiles", [(at, at ^ 1) for at in range(size)]) for factor in mine]
    rows = gather_rows(exchange(requests), count, mine, paired)
    fetched = exchange(rows)
    own, send = contract(requests, fetched, order, tensor_tiles[0], groups)
    total = own.astype(jnp.float32)
    for shift in range(1, groups):
        arrived = lax.ppermute(
            send[shift - 1], "blk", [(i, (i + shift) % groups) for i in range(groups)]
        )
        total = total + arrived.astype(jnp.float32)
    return total


def solution(mesh):
    placed = (
        P("blk", "tiles", None, None),
        P("blk", "tiles"),
        P("blk", "tiles"),
        P("blk", "tiles"),
        P("blk", "tiles"),
        P("blk", "tiles"),
        P(None, "tiles", None),
        P(None, "tiles", None),
    )
    return jax.shard_map(
        per_device, mesh=mesh, in_specs=placed, out_specs=P(("blk", "tiles"), None), check_vma=False
    )
```

profile of v0, /device:TPU:0, one launch (start us, length us, event | category | flops | bytes accessed | tf_op | source)
XLA Modules:
  0.0 30.2 jit_solution(7018620843822995630)
XLA Ops:
  0.0 1.3 %make_requests.1 = (s32[8,1,128]{2,1,0:T(1,128)S(1)}, bf16[256,4,512]{2,1,0:T(4,128)(2,1)S(1)}, bf16[64,4,512]{2,1,0:T(4,128)(2,1)S(1)}) custom-call(s32[1,2]{1,0:T(1,128)} %refs_0_.1, s32[1,2]{1,0:T(1,128)} %refs_1_.1, s32[1,2]{1,0:T(1,128)} %refs_2_.1, s32[1,2]{1,0:T(1,128)} %refs_3_.1, s32[1,2]{1,0:T(1,128)} %refs_4_.1, bf16[256,4,512]{2,1,0:T(4,128)(2,1)} %refs_5_.1, ...), custom_call_target="tpu_custom_call" | custom-call | tf_op jit(solution)/shard_map/make_requests/pallas_call | solution.py:50
  1.3 0.5 %collective-permute-start = (bf16[256,4,512]{2,1,0:T(4,128)(2,1)S(1)}, bf16[256,4,512]{2,1,0:T(4,128)(2,1)S(1)}, u32[]{:S(2)}, u32[]{:S(2)}) collective-permute-start(bf16[256,4,512]{2,1,0:T(4,128)(2,1)S(1)} %get-tuple-element.11.mine_b), channel_id=1, source_target_pairs={{0,1},{1,0},{2,3},{3,2},{4,5},{5,4},{6,7},{7,6},{8,9},{9,8},{10,11... | collective-permute-start | bytes 3145736 | tf_op jit(solution)/shard_map/ppermute | solution.py:174
  1.9 0.1 collective-permute-start.1
  1.9 10.8 %all_to_all.10.asked_ref = s32[8,1,128]{2,1,0:T(1,128)S(1)} all-to-all(s32[8,1,128]{2,1,0:T(1,128)S(1)} %get-tuple-element.10.requests_ref), channel_id=1, replica_groups={{10,12,14,0,2,4,6,8},{11,13,15,1,3,5,7,9},{26,28,30,16,18,20,22,24},{27..., dimensions={0} | all-to-all | bytes 8192 | tf_op jit(solution)/shard_map/all_to_all | solution.py:167
  12.7 0.0 copy-start
  12.7 0.0 collective-permute-done.1.pair_c
  12.7 0.0 collective-permute-done.pair_b
  12.7 0.1 gather_rows.1
  12.9 10.7 %all_to_all.11.fetched_ref = bf16[8,4,2,4,512]{4,3,2,1,0:T(4,128)(2,1)S(1)} all-to-all(bf16[8,4,2,4,512]{4,3,2,1,0:T(4,128)(2,1)S(1)} %gather_rows.1), channel_id=1, replica_groups={{10,12,14,0,2,4,6,8},{11,13,15,1,3,5,7,9},{26,28,30,16,18,20,22,24},{27..., dimensions={0} | all-to-all | bytes 524288 | tf_op jit(solution)/shard_map/all_to_all | solution.py:167
  23.6 0.0 copy-done
  23.6 1.7 %contract.1 = (bf16[64,512]{1,0:T(8,128)(2,1)S(1)}, bf16[1,64,512]{2,1,0:T(8,128)(2,1)S(1)}) custom-call(s32[8,1,128]{2,1,0:T(1,128)S(1)} %get-tuple-element.10.requests_ref, bf16[8,4,2,4,512]{4,3,2,1,0:T(4,128)(2,1)S(1)} %all_to_all.11.fetched_ref, bf16[2,64,4096]{2,1,0:T(8,128)(2,1)S(1)} %bitcast.2), custom_call_target="tpu_custom_call" | custom-call | tf_op jit(solution)/shard_map/contract/pallas_call | solution.py:134
  25.2 1.6 %collective-permute-start.2 = (bf16[64,512]{1,0:T(8,128)(2,1)S(1)}, bf16[64,512]{1,0:T(8,128)(2,1)S(1)}, u32[]{:S(2)}, u32[]{:S(2)}) collective-permute-start(bf16[64,512]{1,0:T(8,128)(2,1)S(1)} %bitcast.3), channel_id=1, source_target_pairs={{0,16},{16,0},{1,17},{17,1},{2,18},{18,2},{3,19},{19,3},{4,20},{20... | collective-permute-start | bytes 196616 | tf_op jit(solution)/shard_map/ppermute | solution.py:180
  26.8 2.7 %collective-permute-done.2 = bf16[64,512]{1,0:T(8,128)(2,1)S(1)} collective-permute-done((bf16[64,512]{1,0:T(8,128)(2,1)S(1)}, bf16[64,512]{1,0:T(8,128)(2,1)S(1)}, u32[]{:S(2)}, u32[]{:S(2)}) %collective-permute-start.2) | collective-permute-done | bytes 65568 | tf_op jit(solution)/shard_map/ppermute | solution.py:180
  29.6 0.7 %convert_add_fusion = f32[64,512]{1,0:T(8,128)} fusion(bf16[64,512]{1,0:T(8,128)(2,1)S(1)} %collective-permute-done.2, bf16[64,512]{1,0:T(8,128)(2,1)S(1)} %get-tuple-element.13), kind=kLoop, calls=%fused_computation | loop fusion | flops 98304 | bytes 262144 | tf_op jit(solution)/shard_map/add | solution.py:183
Async XLA Ops:
  1.3 11.4 %collective-permute-start = (bf16[256,4,512]{2,1,0:T(4,128)(2,1)S(1)}, bf16[256,4,512]{2,1,0:T(4,128)(2,1)S(1)}, u32[]{:S(2)}, u32[]{:S(2)}) collective-permute-start(bf16[256,4,512]{2,1,0:T(4,128)(2,1)S(1)} %get-tuple-element.11.mine_b), channel_id=1, source_target_pairs={{0,1},{1,0},{2,3},{3,2},{4,5},{5,4},{6,7},{7,6},{8,9},{9,8},{10,11... | collective-permute-start | bytes 3145736 | tf_op jit(solution)/shard_map/ppermute | solution.py:174
  1.9 10.9 %collective-permute-start.1 = (bf16[64,4,512]{2,1,0:T(4,128)(2,1)S(1)}, bf16[64,4,512]{2,1,0:T(4,128)(2,1)S(1)}, u32[]{:S(2)}, u32[]{:S(2)}) collective-permute-start(bf16[64,4,512]{2,1,0:T(4,128)(2,1)S(1)} %get-tuple-element.12.mine_c), channel_id=1, source_target_pairs={{0,1},{1,0},{2,3},{3,2},{4,5},{5,4},{6,7},{7,6},{8,9},{9,8},{10,11... | collective-permute-start | bytes 786440 | tf_op jit(solution)/shard_map/ppermute | solution.py:174
  12.7 10.8 %copy-start = (bf16[1,2,64,4096]{3,2,1,0:T(8,128)(2,1)S(1)}, bf16[1,2,64,4096]{3,2,1,0:T(8,128)(2,1)}, u32[]{:S(2)}) copy-start(bf16[1,2,64,4096]{3,2,1,0:T(8,128)(2,1)} %param.8) | copy-start | bytes 3145732
  25.2 4.3 %collective-permute-start.2 = (bf16[64,512]{1,0:T(8,128)(2,1)S(1)}, bf16[64,512]{1,0:T(8,128)(2,1)S(1)}, u32[]{:S(2)}, u32[]{:S(2)}) collective-permute-start(bf16[64,512]{1,0:T(8,128)(2,1)S(1)} %bitcast.3), channel_id=1, source_target_pairs={{0,16},{16,0},{1,17},{17,1},{2,18},{18,2},{3,19},{19,3},{4,20},{20... | collective-permute-start | bytes 196616 | tf_op jit(solution)/shard_map/ppermute | solution.py:180
where the time goes:
time: 30.4 us; the launch traced here: 30.2 us
  blocking collectives  21.5 us (71%)
  Pallas kernels  3.12 us (10%)
  waiting for transfers between devices  2.75 us (9%)
  starting transfers between devices  2.18 us (7%)
  other arithmetic  0.67 us (2%)
    all_to_all x2, blocking collectives, exchange(): lax.all_to_all(array, 'tiles', split_axis=0, concat_axis=0, tiled=True, a...  21.5 us
    ppermute x1, waiting for transfers between devices, per_device(): lax.ppermute(send[shift - 1], 'blk', [(i, (i + shift) % groups) for i in...  2.74 us
    pallas_call x1, Pallas kernels, contract(): pl.pallas_call(kernel, out_shape=(jax.ShapeDtypeStruct((inner, rank), jnp...  1.65 us
    ppermute x1, starting transfers between devices, per_device(): lax.ppermute(send[shift - 1], 'blk', [(i, (i + shift) % groups) for i in...  1.59 us
    pallas_call x1, Pallas kernels, make_requests(): pl.pallas_call(kernel, out_shape=[jax.ShapeDtypeStruct((chips, 1, LANES),...  1.33 us
    add x1, other arithmetic, per_device(): total = total + arrived.astype(jnp.float32)  0.67 us
  transfers between devices with their start and end apart: 3, of which 1 were waited for; matrix products, arithmetic and copies ran while one was open for 0% of the time, Pallas kernels for 0%

commit v1 on v0

--- a/solution.py
+++ b/solution.py
@@ -7,6 +7,7 @@
 
 MIB = 1024 * 1024
 LANES = 128
+BLOCKS_PER_COPY = 32
 
 
 def in_hbm(*arrays):
@@ -18,18 +19,33 @@
     listed = list_two.shape[1]
     small = (owners, slots_two, slots_three, list_two, list_three)
     factors = (factor_b, factor_c)
+    many = [max(1, factor.shape[0] // BLOCKS_PER_COPY) for factor in factors]
+    blocks = sum(factor.shape[0] for factor in factors)
 
     def kernel(*refs):
-        sources, outs, held, sem = refs[:7], refs[7:10], refs[10:15], refs[15]
+        sources, wide, out_ref, staged_ref = refs[:5], refs[5:7], refs[7], refs[8]
+        held, sem, wide_sem = refs[9:14], refs[14], refs[15]
         copies = [
-            pltpu.make_async_copy(source, target, sem.at[at])
-            for at, (source, target) in enumerate(zip(sources, (*held, *outs[1:])))
+            pltpu.make_async_copy(source, target, sem.at[at]) for at, (source, target) in enumerate(zip(sources, held))
         ]
         for copy in copies:
             copy.start()
-        for copy in copies[:5]:
+        staging, first = [], 0
+        for source, parts in zip(wide, many):
+            size = source.shape[0] // parts
+            for part in range(parts):
+                staging.append(
+                    pltpu.make_async_copy(
+                        source.at[pl.ds(part * size, size)],
+                        staged_ref.at[pl.ds(first + part * size, size)],
+                        wide_sem.at[len(staging)],
+                    )
+                )
+                staging[-1].start()
+            first += source.shape[0]
+        for copy in copies:
             copy.wait()
-        own, slot_two, slot_three, two, three = held
+        own, slot_two, slot_three, two, three = (ref[...] for ref in held)
         words = []
         for slot, table in ((slot_two, two), (slot_three, three)):
             for which in range(count):
@@ -43,45 +59,47 @@
         for at, word in enumerate(words):
             row = jnp.where(lane == at, word, row)
         for chip in range(chips):
-            outs[0][chip] = row
-        for copy in copies[5:]:
+            out_ref[chip] = row
+        for copy in staging:
             copy.wait()
 
     return pl.pallas_call(
         kernel,
-        out_shape=[jax.ShapeDtypeStruct((chips, 1, LANES), jnp.int32)]
-        + [jax.ShapeDtypeStruct(factor.shape, factor.dtype) for factor in factors],
+        out_shape=[
+            jax.ShapeDtypeStruct((chips, 1, LANES), jnp.int32),
+            jax.ShapeDtypeStruct((blocks, *factor_b.shape[1:]), factor_b.dtype),
+        ],
         in_specs=[pl.BlockSpec(memory_space=pltpu.HBM)] * 7,
-        out_specs=[pl.BlockSpec(memory_space=pltpu.VMEM)] * 3,
-        scratch_shapes=[pltpu.SMEM(array.shape, jnp.int32) for array in small] + [pltpu.SemaphoreType.DMA((7,))],
+        out_specs=[pl.BlockSpec(memory_space=pltpu.VMEM)] * 2,
+        scratch_shapes=[pltpu.VMEM(array.shape, jnp.int32) for array in small]
+        + [pltpu.SemaphoreType.DMA((5,)), pltpu.SemaphoreType.DMA((sum(many),))],
         compiler_params=pltpu.CompilerParams(vmem_limit_bytes=8 * MIB),
         name="make_requests",
     )(*in_hbm(*small, *factors))
 
 
-def gather_rows(asked, count, mine, paired):
+def gather_rows(asked, count, first_three, mine, paired):
     chips = asked.shape[0]
     wants = 2 * count
-    rows, rank = mine[0].shape[1:]
-
-    def kernel(asked_ref, mine_b, mine_c, pair_b, pair_c, out_ref):
+    rows, rank = mine.shape[1:]
+
+    def kernel(asked_ref, mine_ref, paired_ref, out_ref):
         side = lax.rem(lax.axis_index("tiles"), 2)
         for chip in range(chips):
             words = asked_ref[chip]
             for want in range(wants):
-                own, other = (mine_b, pair_b) if want < count else (mine_c, pair_c)
-                block = words[0, want]
-                out_ref[chip, want, side] = own[block]
-                out_ref[chip, want, 1 - side] = other[block]
+                block = words[0, want] + (0 if want < count else first_three)
+                out_ref[chip, want, side] = mine_ref[block]
+                out_ref[chip, want, 1 - side] = paired_ref[block]
 
     return pl.pallas_call(
         kernel,
-        out_shape=jax.ShapeDtypeStruct((chips, wants, 2, rows, rank), mine[0].dtype),
-        in_specs=[pl.BlockSpec(memory_space=pltpu.VMEM)] * 5,
+        out_shape=jax.ShapeDtypeStruct((chips, wants, 2, rows, rank), mine.dtype),
+        in_specs=[pl.BlockSpec(memory_space=pltpu.VMEM)] * 3,
         out_specs=pl.BlockSpec(memory_space=pltpu.VMEM),
         compiler_params=pltpu.CompilerParams(vmem_limit_bytes=8 * MIB),
         name="gather_rows",
-    )(asked, *mine, *paired)
+    )(asked, mine, paired)
 
 
 def contract(requests, fetched, order, tiles, groups):
@@ -89,7 +107,7 @@
     count, inner, width = tiles.shape
     across = chips * halves * rows
     depth = width // across
-    step = max(1, 1024 // depth)
+    step = max(1, 256 // depth)
 
     def kernel(requests_ref, fetched_ref, tiles_ref, own_ref, send_ref, factor_ref, index_ref, sem):
         copy = pltpu.make_async_copy(requests_ref.at[0], index_ref, sem)
@@ -168,11 +186,11 @@
             array, "tiles", split_axis=0, concat_axis=0, tiled=True, axis_index_groups=same_side
         )
 
-    requests, *mine = make_requests(
+    requests, mine = make_requests(
         chips, tile_iblock, tile_jslot, tile_kslot, block_jlist, block_klist, factor_b, factor_c
     )
-    paired = [lax.ppermute(factor, "tiles", [(at, at ^ 1) for at in range(size)]) for factor in mine]
-    rows = gather_rows(exchange(requests), count, mine, paired)
+    paired = lax.ppermute(mine, "tiles", [(at, at ^ 1) for at in range(size)])
+    rows = gather_rows(exchange(requests), count, factor_b.shape[0], mine, paired)
     fetched = exchange(rows)
     own, send = contract(requests, fetched, order, tensor_tiles[0], groups)
     total = own.astype(jnp.float32)

time: 30.4 us -> 30.6 us (level)
  transfers between devices with their start and end apart: 3 -> 2, of which waited for: 1 -> 1; matrix products, arithmetic and copies ran while one was open for 0% -> 0% of each run, Pallas kernels for 0% -> 0%
where the time goes in v1:
time: 30.6 us; the launch traced here: 30.3 us
  blocking collectives  21.5 us (70%)
  Pallas kernels  3.32 us (11%)
  waiting for transfers between devices  2.75 us (9%)
  starting transfers between devices  2.1 us (7%)
  other arithmetic  0.67 us (2%)
    all_to_all x2, blocking collectives, exchange(): lax.all_to_all(array, 'tiles', split_axis=0, concat_axis=0, tiled=True, a...  21.5 us
    ppermute x1, waiting for transfers between devices, per_device(): lax.ppermute(send[shift - 1], 'blk', [(i, (i + shift) % groups) for i in...  2.74 us
    pallas_call x1, Pallas kernels, contract(): pl.pallas_call(kernel, out_shape=(jax.ShapeDtypeStruct((inner, rank), jnp...  1.65 us
    ppermute x1, starting transfers between devices, per_device(): lax.ppermute(send[shift - 1], 'blk', [(i, (i + shift) % groups) for i in...  1.59 us
    pallas_call x1, Pallas kernels, make_requests(): pl.pallas_call(kernel, out_shape=[jax.ShapeDtypeStruct((chips, 1, LANES),...  1.53 us
    add x1, other arithmetic, per_device(): total = total + arrived.astype(jnp.float32)  0.67 us
  transfers between devices with their start and end apart: 2, of which 1 were waited for; matrix products, arithmetic and copies ran while one was open for 0% of the time, Pallas kernels for 0%

profile of v1, /device:TPU:0, one launch (start us, length us, event | category | flops | bytes accessed | tf_op | source)
XLA Modules:
  0.0 30.3 jit_solution(4350390696692490194)
XLA Ops:
  0.0 1.5 %make_requests.1 = (s32[8,1,128]{2,1,0:T(1,128)S(1)}, bf16[320,4,512]{2,1,0:T(4,128)(2,1)S(1)}) custom-call(s32[1,2]{1,0:T(1,128)} %refs_0_.1, s32[1,2]{1,0:T(1,128)} %refs_1_.1, s32[1,2]{1,0:T(1,128)} %refs_2_.1, s32[1,2]{1,0:T(1,128)} %refs_3_.1, s32[1,2]{1,0:T(1,128)} %refs_4_.1, bf16[256,4,512]{2,1,0:T(4,128)(2,1)} %refs_5_.1, bf16[64,4,512]{2,1,0:T(4,128)(2,1)} %refs_6_.1), custom_call_target="tpu_custom_call" | custom-call | tf_op jit(solution)/shard_map/make_requests/pallas_call | solution.py:66
  1.5 0.5 %collective-permute-start = (bf16[320,4,512]{2,1,0:T(4,128)(2,1)S(1)}, bf16[320,4,512]{2,1,0:T(4,128)(2,1)S(1)}, u32[]{:S(2)}, u32[]{:S(2)}) collective-permute-start(bf16[320,4,512]{2,1,0:T(4,128)(2,1)S(1)} %get-tuple-element.10.mine_ref), channel_id=1, source_target_pairs={{0,1},{1,0},{2,3},{3,2},{4,5},{5,4},{6,7},{7,6},{8,9},{9,8},{10,11... | collective-permute-start | bytes 3932168 | tf_op jit(solution)/shard_map/ppermute | solution.py:192
  2.1 10.4 %all_to_all.10.asked_ref = s32[8,1,128]{2,1,0:T(1,128)S(1)} all-to-all(s32[8,1,128]{2,1,0:T(1,128)S(1)} %get-tuple-element.9.requests_ref), channel_id=1, replica_groups={{10,12,14,0,2,4,6,8},{11,13,15,1,3,5,7,9},{26,28,30,16,18,20,22,24},{27..., dimensions={0} | all-to-all | bytes 8192 | tf_op jit(solution)/shard_map/all_to_all | solution.py:185
  12.4 0.0 copy-start
  12.4 0.0 collective-permute-done.paired_ref
  12.4 0.1 gather_rows.1
  12.6 11.1 %all_to_all.11.fetched_ref = bf16[8,4,2,4,512]{4,3,2,1,0:T(4,128)(2,1)S(1)} all-to-all(bf16[8,4,2,4,512]{4,3,2,1,0:T(4,128)(2,1)S(1)} %gather_rows.1), channel_id=1, replica_groups={{10,12,14,0,2,4,6,8},{11,13,15,1,3,5,7,9},{26,28,30,16,18,20,22,24},{27..., dimensions={0} | all-to-all | bytes 524288 | tf_op jit(solution)/shard_map/all_to_all | solution.py:185
  23.7 0.0 copy-done
  23.7 1.7 %contract.1 = (bf16[64,512]{1,0:T(8,128)(2,1)S(1)}, bf16[1,64,512]{2,1,0:T(8,128)(2,1)S(1)}) custom-call(s32[8,1,128]{2,1,0:T(1,128)S(1)} %get-tuple-element.9.requests_ref, bf16[8,4,2,4,512]{4,3,2,1,0:T(4,128)(2,1)S(1)} %all_to_all.11.fetched_ref, bf16[2,64,4096]{2,1,0:T(8,128)(2,1)S(1)} %bitcast.2), custom_call_target="tpu_custom_call" | custom-call | tf_op jit(solution)/shard_map/contract/pallas_call | solution.py:152
  25.3 1.6 %collective-permute-start.1 = (bf16[64,512]{1,0:T(8,128)(2,1)S(1)}, bf16[64,512]{1,0:T(8,128)(2,1)S(1)}, u32[]{:S(2)}, u32[]{:S(2)}) collective-permute-start(bf16[64,512]{1,0:T(8,128)(2,1)S(1)} %bitcast.3), channel_id=1, source_target_pairs={{0,16},{16,0},{1,17},{17,1},{2,18},{18,2},{3,19},{19,3},{4,20},{20... | collective-permute-start | bytes 196616 | tf_op jit(solution)/shard_map/ppermute | solution.py:198
  26.9 2.7 %collective-permute-done.1 = bf16[64,512]{1,0:T(8,128)(2,1)S(1)} collective-permute-done((bf16[64,512]{1,0:T(8,128)(2,1)S(1)}, bf16[64,512]{1,0:T(8,128)(2,1)S(1)}, u32[]{:S(2)}, u32[]{:S(2)}) %collective-permute-start.1) | collective-permute-done | bytes 65568 | tf_op jit(solution)/shard_map/ppermute | solution.py:198
  29.7 0.7 %convert_add_fusion = f32[64,512]{1,0:T(8,128)} fusion(bf16[64,512]{1,0:T(8,128)(2,1)S(1)} %collective-permute-done.1, bf16[64,512]{1,0:T(8,128)(2,1)S(1)} %get-tuple-element.11), kind=kLoop, calls=%fused_computation | loop fusion | flops 98304 | bytes 262144 | tf_op jit(solution)/shard_map/add | solution.py:201
Async XLA Ops:
  1.5 10.9 %collective-permute-start = (bf16[320,4,512]{2,1,0:T(4,128)(2,1)S(1)}, bf16[320,4,512]{2,1,0:T(4,128)(2,1)S(1)}, u32[]{:S(2)}, u32[]{:S(2)}) collective-permute-start(bf16[320,4,512]{2,1,0:T(4,128)(2,1)S(1)} %get-tuple-element.10.mine_ref), channel_id=1, source_target_pairs={{0,1},{1,0},{2,3},{3,2},{4,5},{5,4},{6,7},{7,6},{8,9},{9,8},{10,11... | collective-permute-start | bytes 3932168 | tf_op jit(solution)/shard_map/ppermute | solution.py:192
  12.4 11.2 %copy-start = (bf16[1,2,64,4096]{3,2,1,0:T(8,128)(2,1)S(1)}, bf16[1,2,64,4096]{3,2,1,0:T(8,128)(2,1)}, u32[]{:S(2)}) copy-start(bf16[1,2,64,4096]{3,2,1,0:T(8,128)(2,1)} %param.8) | copy-start | bytes 3145732
  25.3 4.3 %collective-permute-start.1 = (bf16[64,512]{1,0:T(8,128)(2,1)S(1)}, bf16[64,512]{1,0:T(8,128)(2,1)S(1)}, u32[]{:S(2)}, u32[]{:S(2)}) collective-permute-start(bf16[64,512]{1,0:T(8,128)(2,1)S(1)} %bitcast.3), channel_id=1, source_target_pairs={{0,16},{16,0},{1,17},{17,1},{2,18},{18,2},{3,19},{19,3},{4,20},{20... | collective-permute-start | bytes 196616 | tf_op jit(solution)/shard_map/ppermute | solution.py:198

commit v2 on v1

--- a/solution.py
+++ b/solution.py
@@ -7,7 +7,7 @@
 
 MIB = 1024 * 1024
 LANES = 128
-BLOCKS_PER_COPY = 32
+BLOCKS_PER_COPY = 256
 
 
 def in_hbm(*arrays):

time: 30.6 us -> 30.4 us (level)
  no operation moved by 1% of the time
where the time goes in v2:
time: 30.4 us; the launch traced here: 30.2 us
  blocking collectives  21.5 us (71%)
  Pallas kernels  3.2 us (11%)
  waiting for transfers between devices  2.75 us (9%)
  starting transfers between devices  2.1 us (7%)
  other arithmetic  0.67 us (2%)
    all_to_all x2, blocking collectives, exchange(): lax.all_to_all(array, 'tiles', split_axis=0, concat_axis=0, tiled=True, a...  21.5 us
    ppermute x1, waiting for transfers between devices, per_device(): lax.ppermute(send[shift - 1], 'blk', [(i, (i + shift) % groups) for i in...  2.74 us
    pallas_call x1, Pallas kernels, contract(): pl.pallas_call(kernel, out_shape=(jax.ShapeDtypeStruct((inner, rank), jnp...  1.65 us
    ppermute x1, starting transfers between devices, per_device(): lax.ppermute(send[shift - 1], 'blk', [(i, (i + shift) % groups) for i in...  1.59 us
    pallas_call x1, Pallas kernels, make_requests(): pl.pallas_call(kernel, out_shape=[jax.ShapeDtypeStruct((chips, 1, LANES),...  1.41 us
    add x1, other arithmetic, per_device(): total = total + arrived.astype(jnp.float32)  0.67 us
  transfers between devices with their start and end apart: 2, of which 1 were waited for; matrix products, arithmetic and copies ran while one was open for 0% of the time, Pallas kernels for 0%

profile of v2, /device:TPU:0, one launch (start us, length us, event | category | flops | bytes accessed | tf_op | source)
XLA Modules:
  0.0 30.2 jit_solution(3703526106709911667)
XLA Ops:
  0.0 1.4 %make_requests.1 = (s32[8,1,128]{2,1,0:T(1,128)S(1)}, bf16[320,4,512]{2,1,0:T(4,128)(2,1)S(1)}) custom-call(s32[1,2]{1,0:T(1,128)} %refs_0_.1, s32[1,2]{1,0:T(1,128)} %refs_1_.1, s32[1,2]{1,0:T(1,128)} %refs_2_.1, s32[1,2]{1,0:T(1,128)} %refs_3_.1, s32[1,2]{1,0:T(1,128)} %refs_4_.1, bf16[256,4,512]{2,1,0:T(4,128)(2,1)} %refs_5_.1, bf16[64,4,512]{2,1,0:T(4,128)(2,1)} %refs_6_.1), custom_call_target="tpu_custom_call" | custom-call | tf_op jit(solution)/shard_map/make_requests/pallas_call | solution.py:66
  1.4 0.5 %collective-permute-start = (bf16[320,4,512]{2,1,0:T(4,128)(2,1)S(1)}, bf16[320,4,512]{2,1,0:T(4,128)(2,1)S(1)}, u32[]{:S(2)}, u32[]{:S(2)}) collective-permute-start(bf16[320,4,512]{2,1,0:T(4,128)(2,1)S(1)} %get-tuple-element.10.mine_ref), channel_id=1, source_target_pairs={{0,1},{1,0},{2,3},{3,2},{4,5},{5,4},{6,7},{7,6},{8,9},{9,8},{10,11... | collective-permute-start | bytes 3932168 | tf_op jit(solution)/shard_map/ppermute | solution.py:192
  1.9 10.4 %all_to_all.10.asked_ref = s32[8,1,128]{2,1,0:T(1,128)S(1)} all-to-all(s32[8,1,128]{2,1,0:T(1,128)S(1)} %get-tuple-element.9.requests_ref), channel_id=1, replica_groups={{10,12,14,0,2,4,6,8},{11,13,15,1,3,5,7,9},{26,28,30,16,18,20,22,24},{27..., dimensions={0} | all-to-all | bytes 8192 | tf_op jit(solution)/shard_map/all_to_all | solution.py:185
  12.3 0.0 copy-start
  12.3 0.0 collective-permute-done.paired_ref
  12.3 0.1 gather_rows.1
  12.5 11.1 %all_to_all.11.fetched_ref = bf16[8,4,2,4,512]{4,3,2,1,0:T(4,128)(2,1)S(1)} all-to-all(bf16[8,4,2,4,512]{4,3,2,1,0:T(4,128)(2,1)S(1)} %gather_rows.1), channel_id=1, replica_groups={{10,12,14,0,2,4,6,8},{11,13,15,1,3,5,7,9},{26,28,30,16,18,20,22,24},{27..., dimensions={0} | all-to-all | bytes 524288 | tf_op jit(solution)/shard_map/all_to_all | solution.py:185
  23.6 0.0 copy-done
  23.6 1.7 %contract.1 = (bf16[64,512]{1,0:T(8,128)(2,1)S(1)}, bf16[1,64,512]{2,1,0:T(8,128)(2,1)S(1)}) custom-call(s32[8,1,128]{2,1,0:T(1,128)S(1)} %get-tuple-element.9.requests_ref, bf16[8,4,2,4,512]{4,3,2,1,0:T(4,128)(2,1)S(1)} %all_to_all.11.fetched_ref, bf16[2,64,4096]{2,1,0:T(8,128)(2,1)S(1)} %bitcast.2), custom_call_target="tpu_custom_call" | custom-call | tf_op jit(solution)/shard_map/contract/pallas_call | solution.py:152
  25.2 1.6 %collective-permute-start.1 = (bf16[64,512]{1,0:T(8,128)(2,1)S(1)}, bf16[64,512]{1,0:T(8,128)(2,1)S(1)}, u32[]{:S(2)}, u32[]{:S(2)}) collective-permute-start(bf16[64,512]{1,0:T(8,128)(2,1)S(1)} %bitcast.3), channel_id=1, source_target_pairs={{0,16},{16,0},{1,17},{17,1},{2,18},{18,2},{3,19},{19,3},{4,20},{20... | collective-permute-start | bytes 196616 | tf_op jit(solution)/shard_map/ppermute | solution.py:198
  26.8 2.7 %collective-permute-done.1 = bf16[64,512]{1,0:T(8,128)(2,1)S(1)} collective-permute-done((bf16[64,512]{1,0:T(8,128)(2,1)S(1)}, bf16[64,512]{1,0:T(8,128)(2,1)S(1)}, u32[]{:S(2)}, u32[]{:S(2)}) %collective-permute-start.1) | collective-permute-done | bytes 65568 | tf_op jit(solution)/shard_map/ppermute | solution.py:198
  29.5 0.7 %convert_add_fusion = f32[64,512]{1,0:T(8,128)} fusion(bf16[64,512]{1,0:T(8,128)(2,1)S(1)} %collective-permute-done.1, bf16[64,512]{1,0:T(8,128)(2,1)S(1)} %get-tuple-element.11), kind=kLoop, calls=%fused_computation | loop fusion | flops 98304 | bytes 262144 | tf_op jit(solution)/shard_map/add | solution.py:201
Async XLA Ops:
  1.4 10.9 %collective-permute-start = (bf16[320,4,512]{2,1,0:T(4,128)(2,1)S(1)}, bf16[320,4,512]{2,1,0:T(4,128)(2,1)S(1)}, u32[]{:S(2)}, u32[]{:S(2)}) collective-permute-start(bf16[320,4,512]{2,1,0:T(4,128)(2,1)S(1)} %get-tuple-element.10.mine_ref), channel_id=1, source_target_pairs={{0,1},{1,0},{2,3},{3,2},{4,5},{5,4},{6,7},{7,6},{8,9},{9,8},{10,11... | collective-permute-start | bytes 3932168 | tf_op jit(solution)/shard_map/ppermute | solution.py:192
  12.3 11.2 %copy-start = (bf16[1,2,64,4096]{3,2,1,0:T(8,128)(2,1)S(1)}, bf16[1,2,64,4096]{3,2,1,0:T(8,128)(2,1)}, u32[]{:S(2)}) copy-start(bf16[1,2,64,4096]{3,2,1,0:T(8,128)(2,1)} %param.8) | copy-start | bytes 3145732
  25.2 4.3 %collective-permute-start.1 = (bf16[64,512]{1,0:T(8,128)(2,1)S(1)}, bf16[64,512]{1,0:T(8,128)(2,1)S(1)}, u32[]{:S(2)}, u32[]{:S(2)}) collective-permute-start(bf16[64,512]{1,0:T(8,128)(2,1)S(1)} %bitcast.3), channel_id=1, source_target_pairs={{0,16},{16,0},{1,17},{17,1},{2,18},{18,2},{3,19},{19,3},{4,20},{20... | collective-permute-start | bytes 196616 | tf_op jit(solution)/shard_map/ppermute | solution.py:198
